TPU v7x, 512 devices: a whole 4x4x16 slice. The times are simulated.
512 devices in a mesh: dp: 8 (over x, z_hi), ctx: 64 (over y, z_lo, core).
Axes of the slice: x: 4, y: 4, z: 16 (z_hi: 2, z_lo: 8; z = z_hi * 8 + z_lo), core: 2. Of those that a mesh axis runs over, the one named last changes fastest.
Arguments:
- inputs: float32 [8, 2048, 8192], P('dp', None, 'ctx'), may hold values from -6 to 6
- grad_out: float32 [8, 2048, 8192], P('dp', None, 'ctx'), may hold values from -6 to 6
- filters: float32 [2048, 8192], P(('dp', 'ctx')), may hold values from -0.0625 to 0.0625
Outputs:
- input_grad: float32 [8, 2048, 8192], P('dp', None, 'ctx')
- filter_grad: float32 [2048, 8192], P(('dp', 'ctx'))
All inputs are finite; a program needn't handle non-finite values.
Results may differ from a plain program's by a relative error of at most 0.000098.
Values sent between devices are 32-bit elements; how exact they have to be, the bound alone decides.
No kernel may reach another device: no remote copies, remote signals or barrier semaphores. Data moves between devices by JAX's collectives and lax.ppermute only.
A program may use at most 64 MiB of HBM per device.

v0:
```python
import math
import jax
import jax.numpy as jnp
from jax import lax
from jax.sharding import PartitionSpec as P


def dft_tables(seq_length):
    inner_size = 128
    padded_size = 2 * seq_length
    outer_size = padded_size // inner_size
    signal_rows = seq_length // inner_size
    freq_count = outer_size // 2 + 1
    two_pi = 2.0 * math.pi
    order_rows = jnp.arange(signal_rows, dtype=jnp.int32)
    order_freq = jnp.arange(freq_count, dtype=jnp.int32)
    order_inner = jnp.arange(inner_size, dtype=jnp.int32)
    angle_outer = (
        two_pi
        / outer_size
        * (order_rows[:, None] * order_freq[None, :] % outer_size).astype(jnp.float32)
    )
    cos_outer = jnp.cos(angle_outer)
    sin_outer = jnp.sin(angle_outer)
    first_table = jnp.concatenate([cos_outer, -sin_outer], axis=1)
    weights = jnp.where((order_freq == 0) | (order_freq == freq_count - 1), 1.0, 2.0).astype(
        jnp.float32
    )
    last_table = jnp.concatenate(
        [(cos_outer * weights[None, :]).T, (-sin_outer * weights[None, :]).T], axis=0
    )
    angle_inner = (
        two_pi
        / inner_size
        * (order_inner[:, None] * order_inner[None, :] % inner_size).astype(jnp.float32)
    )
    cos_inner = jnp.cos(angle_inner)
    sin_inner = jnp.sin(angle_inner)
    forward_block = jnp.concatenate(
        [
            jnp.concatenate([cos_inner, -sin_inner], axis=1),
            jnp.concatenate([sin_inner, cos_inner], axis=1),
        ],
        axis=0,
    )
    inverse_block = jnp.concatenate(
        [
            jnp.concatenate([cos_inner, sin_inner], axis=1),
            jnp.concatenate([-sin_inner, cos_inner], axis=1),
        ],
        axis=0,
    )
    angle_turn = (
        two_pi
        / padded_size
        * (order_freq[:, None] * order_inner[None, :] % padded_size).astype(jnp.float32)
    )
    return (
        first_table,
        last_table,
        forward_block,
        inverse_block,
        jnp.cos(angle_turn),
        jnp.sin(angle_turn),
        freq_count,
        signal_rows,
        padded_size,
    )


def forward_spectrum(signal, tables):
    (
        first_table,
        last_table,
        forward_block,
        inverse_block,
        cos_turn,
        sin_turn,
        freq_count,
        signal_rows,
        padded_size,
    ) = tables
    highest = lax.Precision.HIGHEST
    row_count = signal.shape[0]
    shaped = signal.reshape(row_count, signal_rows, 128)
    first = jnp.einsum("man,ak->mkn", shaped, first_table, precision=highest)
    first_real = first[:, :freq_count]
    first_imag = first[:, freq_count:]
    turned = jnp.concatenate(
        [
            first_real * cos_turn + first_imag * sin_turn,
            first_imag * cos_turn - first_real * sin_turn,
        ],
        axis=-1,
    )
    return jnp.einsum("mkn,nj->mkj", turned, forward_block, precision=highest)


def inverse_signal(spec_real, spec_imag, tables):
    (
        first_table,
        last_table,
        forward_block,
        inverse_block,
        cos_turn,
        sin_turn,
        freq_count,
        signal_rows,
        padded_size,
    ) = tables
    highest = lax.Precision.HIGHEST
    row_count = spec_real.shape[0]
    stacked = jnp.concatenate([spec_real, spec_imag], axis=-1)
    middle = jnp.einsum("mkj,jn->mkn", stacked, inverse_block, precision=highest)
    middle_real = middle[..., :128]
    middle_imag = middle[..., 128:]
    back = jnp.concatenate(
        [
            middle_real * cos_turn - middle_imag * sin_turn,
            middle_imag * cos_turn + middle_real * sin_turn,
        ],
        axis=1,
    )
    result = jnp.einsum("mkn,ka->man", back, last_table, precision=highest)
    return (result / padded_size).reshape(row_count, -1)


def shards(inputs, grad_out, filters):
    dp_count = lax.axis_size("dp")
    ctx_count = lax.axis_size("ctx")
    seq_local, channel_count, local_tokens = inputs.shape
    owned_channels = channel_count // (dp_count * ctx_count)
    seq_length = local_tokens * ctx_count
    tables = dft_tables(seq_length)
    freq_count = tables[6]
    split_shape = (seq_local, dp_count, ctx_count, owned_channels, local_tokens)
    split_input = inputs.reshape(split_shape)
    split_grad = grad_out.reshape(split_shape)
    norm_factor = 1.0 / math.sqrt(seq_local * dp_count * seq_length)
    moved_input, moved_grad = (
        lax.all_to_all(split_input, "ctx", split_axis=2, concat_axis=4, tiled=True),
        lax.all_to_all(split_grad, "ctx", split_axis=2, concat_axis=4, tiled=True),
    )
    channels = dp_count * owned_channels
    filter_rows = lax.all_gather(filters, "dp", axis=0, tiled=True)
    spec_shape = (seq_local, channels, freq_count, 256)
    input_spec = forward_spectrum(
        moved_input.reshape(seq_local * channels, seq_length), tables
    ).reshape(spec_shape)
    grad_spec = forward_spectrum(
        moved_grad.reshape(seq_local * channels, seq_length), tables
    ).reshape(spec_shape)
    filter_spec = forward_spectrum(filter_rows, tables)[None]
    input_real = input_spec[..., :128]
    input_imag = input_spec[..., 128:]
    grad_real = grad_spec[..., :128]
    grad_imag = grad_spec[..., 128:]
    filter_real = filter_spec[..., :128]
    filter_imag = filter_spec[..., 128:]
    product_real = grad_real * filter_real + grad_imag * filter_imag
    product_imag = grad_imag * filter_real - grad_real * filter_imag
    input_part = inverse_signal(
        product_real.reshape(seq_local * channels, freq_count, 128),
        product_imag.reshape(seq_local * channels, freq_count, 128),
        tables,
    )
    corr_real = jnp.sum(grad_real * input_real + grad_imag * input_imag, axis=0)
    corr_imag = jnp.sum(grad_imag * input_real - grad_real * input_imag, axis=0)
    filter_part = inverse_signal(corr_real, corr_imag, tables) * norm_factor
    leaving = input_part.reshape(seq_local, dp_count, 1, owned_channels, seq_length)
    returned = lax.all_to_all(leaving, "ctx", split_axis=4, concat_axis=2, tiled=True)
    summed = lax.psum_scatter(
        filter_part.reshape(dp_count, owned_channels, seq_length),
        "dp",
        scatter_dimension=0,
        tiled=True,
    )
    filter_grad = summed.reshape(owned_channels, seq_length)
    input_grad = returned.reshape(seq_local, channel_count, local_tokens)
    return (input_grad, filter_grad)


def solution(mesh):
    placed = (P("dp", None, "ctx"), P("dp", None, "ctx"), P(("dp", "ctx"), None))
    return jax.shard_map(
        shards,
        mesh=mesh,
        in_specs=placed,
        out_specs=(P("dp", None, "ctx"), P(("dp", "ctx"), None)),
        check_vma=False,
    )
```

profile of v0, /device:TPU:14, one launch (start us, length us, event | category | flops | bytes accessed | tf_op | source)
XLA Modules:
  0.0 565.3 jit_solution(7946573195563729075)
XLA Ops:
  7.2 2.5 copy.18
  9.7 16.3 %all-to-all-start = ((f32[1,8,64,4,128]{4,3,1,0,2:T(4,128)}), f32[1,8,64,4,128]{4,3,1,0,2:T(4,128)S(1)}, u32[]{:S(2)}, u32[]{:S(2)}) async-start(f32[1,8,64,4,128]{4,3,1,0,2:T(4,128)} %copy.18), calls=%async_computation | async-start | bytes 2097152 | tf_op jit(solution)/shard_map/all_to_all | solution.py:142
  26.0 1.3 copy.22
  27.3 49.3 %all-to-all-done = f32[1,8,64,4,128]{4,3,1,0,2:T(4,128)S(1)} async-done(((f32[1,8,64,4,128]{4,3,1,0,2:T(4,128)}), f32[1,8,64,4,128]{4,3,1,0,2:T(4,128)S(1)}, u32[]{:S(2)}, u32[]{:S(2)}) %all-to-all-start) | async-done | bytes 1048608 | tf_op jit(solution)/shard_map/all_to_all | solution.py:142
  76.6 9.0 %all-to-all-start.2 = ((f32[1,8,64,4,128]{4,3,1,0,2:T(4,128)}), f32[1,8,64,4,128]{4,3,1,0,2:T(4,128)}, u32[]{:S(2)}, u32[]{:S(2)}) async-start(f32[1,8,64,4,128]{4,3,1,0,2:T(4,128)} %copy.22), calls=%async_computation.2 | async-start | bytes 2097152 | tf_op jit(solution)/shard_map/all_to_all | solution.py:141
  85.6 0.3 all-gather.3.cloned.1.call-start
  85.9 0.4 all-gather.3.cloned.1.call-update
  86.4 0.1 sine_negate_fusion
  86.5 0.3 fusion.84
  86.8 0.8 fusion.85
  87.6 0.3 fusion.76
  87.9 0.8 cosine_multiply_fusion
  88.7 99.1 %all-gather.3.cloned.1.call-done = f32[8,4,8192]{2,1,0:T(4,128)} async-done(((f32[1,4,8192]{2,1,0:T(4,128)}), f32[8,4,8192]{2,1,0:T(4,128)}) %all-gather.3.cloned.1.call-update) | async-done | bytes 1048592 | tf_op jit(solution)/shard_map/all_gather | solution.py:145
  187.7 1.9 reshape.87
  189.7 2.0 convolution_bitcast_fusion.1
  191.7 0.6 copy.19
  192.3 3.4 convolution_bitcast_fusion.2
  195.7 0.0 all-to-all-done.2
  195.7 1.8 copy.23
  197.6 0.0 copy-start.4
  197.6 2.0 convolution_bitcast_fusion
  199.6 0.9 multiply_add_fusion.1
  200.6 2.6 fusion.31
  203.1 2.1 fusion.34
  205.2 2.1 fusion.28
  207.3 0.8 add_bitcast_fusion
  208.1 2.1 fusion.8
  210.2 2.1 fusion.16
  212.3 0.5 multiply_subtract_fusion
  212.8 0.2 copy-done.6
  213.0 0.0 copy-done.7
  213.1 2.4 fusion.46
  215.5 1.6 reshape_reshape.10
  217.2 10.7 %copy.20 = f32[1,8,1,4,8192]{1,3,2,0,4:T(4,128)} copy(f32[1,8,1,4,8192]{4,3,1,2,0:T(4,128)S(1)} %reshape_reshape.10) | data formatting | bytes 2097152 | tf_op jit(solution)/shard_map/reshape;reshape | solution.py:170
  227.9 22.0 %reshape.102 = f32[64,1,4096]{2,1,0:T(1,128)} reshape(f32[8192,1,1,4,8]{4,3,2,1,0:T(4,128)} %bitcast.65) | data formatting | bytes 2097152
  249.8 5.8 %all-to-all-start.1 = ((f32[64,1,4096]{2,1,0:T(1,128)}), f32[64,1,4096]{2,1,0:T(1,128)S(1)}, u32[]{:S(2)}, u32[]{:S(2)}) async-start(f32[64,1,4096]{2,1,0:T(1,128)} %reshape.102), calls=%async_computation.1 | async-start | bytes 2097152 | tf_op jit(solution)/shard_map/all_to_all | solution.py:171
  255.6 0.0 all-reduce.3.cloned.1.call-start
  255.6 2.4 fusion.40
  258.1 2.6 mul.580
  260.7 0.0 all-reduce.3.cloned.1.call-update
  260.7 1.3 dynamic-slice
  262.1 256.1 %all-reduce.3.cloned.1.call-done = f32[8,4,8192]{2,1,0:T(4,128)} async-done(((f32[8,4,8192]{2,1,0:T(4,128)}), f32[8,4,8192]{2,1,0:T(4,128)}) %all-reduce.3.cloned.1.call-update) | async-done | bytes 1048592
  518.1 2.2 dynamic-slice_bitcast_fusion
  520.3 0.0 all-to-all-done.1
  520.3 0.5 broadcast.142
  520.8 3.3 reduce
  524.1 21.2 %reshape.103 = f32[8192,1,1,4,8]{4,3,2,1,0:T(4,128)} reshape(f32[64,4096]{1,0:T(8,128)S(1)} %reduce) | data formatting | bytes 2097152
  545.3 13.0 %copy.21 = f32[1,8,64,1,4,128]{5,4,2,1,3,0:T(4,128)} copy(f32[1,8,64,1,4,128]{1,4,5,2,3,0:T(4,128)} %bitcast.66) | data formatting | bytes 2097152 | tf_op jit(solution)/shard_map/all_to_all | solution.py:171
  (14 shorter events, 0.0 us)
Async XLA Ops:
  9.7 16.3 %copy-start.3 = (f32[1,2048,128]{2,1,0:T(8,128)S(1)}, f32[1,2048,128]{2,1,0:T(8,128)}, u32[]{:S(2)}) copy-start(f32[1,2048,128]{2,1,0:T(8,128)} %param.3) | copy-start | bytes 3145732
  9.7 66.9 %all-to-all-start = ((f32[1,8,64,4,128]{4,3,1,0,2:T(4,128)}), f32[1,8,64,4,128]{4,3,1,0,2:T(4,128)S(1)}, u32[]{:S(2)}, u32[]{:S(2)}) async-start(f32[1,8,64,4,128]{4,3,1,0,2:T(4,128)} %copy.18), calls=%async_computation | async-start | bytes 2097152 | tf_op jit(solution)/shard_map/all_to_all | solution.py:142
  76.6 10.2 %copy-start.1 = (f32[1,8,64,4,128]{4,3,1,0,2:T(4,128)}, f32[1,8,64,4,128]{4,3,1,0,2:T(4,128)S(1)}, u32[]{:S(2)}) copy-start(f32[1,8,64,4,128]{4,3,1,0,2:T(4,128)S(1)} %all-to-all-done) | copy-start | bytes 3145732
  76.6 119.1 %all-to-all-start.2 = ((f32[1,8,64,4,128]{4,3,1,0,2:T(4,128)}), f32[1,8,64,4,128]{4,3,1,0,2:T(4,128)}, u32[]{:S(2)}, u32[]{:S(2)}) async-start(f32[1,8,64,4,128]{4,3,1,0,2:T(4,128)} %copy.22), calls=%async_computation.2 | async-start | bytes 2097152 | tf_op jit(solution)/shard_map/all_to_all | solution.py:141
  85.6 102.1 %all-gather.3.cloned.1.call-start = ((), (), s32[]{:S(2)}) async-start(), calls=%async_computation.3 | async-start | bytes 1179648 | tf_op jit(solution)/shard_map/all_gather | solution.py:145
  189.7 2.0 copy-start.2
  197.6 2.1 copy-start
  197.6 2.1 copy-start.4
  197.6 2.1 copy-start.5
  212.3 0.8 copy-start.6
  212.3 0.8 copy-start.7
  249.8 270.5 %all-to-all-start.1 = ((f32[64,1,4096]{2,1,0:T(1,128)}), f32[64,1,4096]{2,1,0:T(1,128)S(1)}, u32[]{:S(2)}, u32[]{:S(2)}) async-start(f32[64,1,4096]{2,1,0:T(1,128)} %reshape.102), calls=%async_computation.1 | async-start | bytes 2097152 | tf_op jit(solution)/shard_map/all_to_all | solution.py:171
  255.6 262.5 %all-reduce.3.cloned.1.call-start = ((), (), s32[]{:S(2)}) async-start(), calls=%async_computation.4 | async-start | bytes 2097152
Sparse Core Ops, SparseCore 0:
  89.7 97.9 all-gather.2
  260.9 257.2 all-reduce.2
where the time goes:
time: 569 us; the launch traced here: 565 us
  waiting for transfers between devices  405 us (71%)
  local copies, waits for them, and re-layouts  83.6 us (15%)
  starting transfers between devices  31.4 us (6%)
  matrix products  23.2 us (4%)
  between operations  14.5 us (3%)
  other arithmetic  7.71 us (1%)
    unnamed x3, waiting for transfers between devices  256 us
    all_gather x1, waiting for transfers between devices, shards(): filter_rows = lax.all_gather(filters, 'dp', axis=0, tiled=True)  99.1 us
    all_to_all x1, waiting for transfers between devices, shards(): lax.all_to_all(split_grad, 'ctx', split_axis=2, concat_axis=4, tiled=True)  49.3 us
    unnamed x19, local copies, waits for them, and re-layouts  44.8 us
    all_to_all x1, starting transfers between devices, shards(): lax.all_to_all(split_grad, 'ctx', split_axis=2, concat_axis=4, tiled=True)  16.3 us
    all_to_all x2, local copies, waits for them, and re-layouts, shards(): lax.all_to_all(leaving, 'ctx', split_axis=4, concat_axis=2, tiled=True)  13.5 us
    another operation x2, local copies, waits for them, and re-layouts, shards(): input_part.reshape(seq_local, dp_count, 1, owned_channels, seq_length)  12.3 us
  transfers between devices with their start and end apart: 5, of which 3 were waited for; matrix products, arithmetic and copies ran while one was open for 4% of the time, Pallas kernels for 0%

commit v1 on v0

--- a/solution.py
+++ b/solution.py
@@ -168,7 +168,10 @@
     corr_imag = jnp.sum(grad_imag * input_real - grad_real * input_imag, axis=0)
     filter_part = inverse_signal(corr_real, corr_imag, tables) * norm_factor
     leaving = input_part.reshape(seq_local, dp_count, 1, owned_channels, seq_length)
-    returned = lax.all_to_all(leaving, "ctx", split_axis=4, concat_axis=2, tiled=True)
+    returned = jnp.concatenate(
+        lax.all_to_all(jnp.stack(jnp.split(leaving, lax.axis_size("ctx"), axis=4)), "ctx", 0, 0),
+        axis=2,
+    )
     summed = lax.psum_scatter(
         filter_part.reshape(dp_count, owned_channels, seq_length),
         "dp",

time: 569 us -> 582 us (1.023)
  local copies, waits for them, and re-layouts: 83.6 us -> 101 us
    unnamed x19 -> x80, local copies, waits for them, and re-layouts: 44.8 us -> 84.5 us
    all_to_all x2 -> x0, local copies, waits for them, and re-layouts: 13.5 us -> none  [shards(): lax.all_to_all(leaving, 'ctx', split_axis=4, concat_axis=2, tiled=True)]
    another operation x2 -> x1, local copies, waits for them, and re-layouts: 12.3 us -> 1.39 us  [shards(): input_part.reshape(seq_local, dp_count, 1, owned_channels, seq_length)]
  transfers between devices with their start and end apart: 5 -> 5, of which waited for: 3 -> 3; matrix products, arithmetic and copies ran while one was open for 4% -> 3% of each run, Pallas kernels for 0% -> 0%
where the time goes in v1:
time: 582 us; the launch traced here: 578 us
  waiting for transfers between devices  404 us (69%)
  local copies, waits for them, and re-layouts  101 us (17%)
  starting transfers between devices  31.3 us (5%)
  matrix products  22 us (4%)
  between operations  14.3 us (2%)
    unnamed x3, waiting for transfers between devices  256 us
    all_gather x1, waiting for transfers between devices, shards(): filter_rows = lax.all_gather(filters, 'dp', axis=0, tiled=True)  99.1 us
    unnamed x80, local copies, waits for them, and re-layouts  84.5 us
    all_to_all x1, waiting for transfers between devices, shards(): lax.all_to_all(split_grad, 'ctx', split_axis=2, concat_axis=4, tiled=True)  49.3 us
    all_to_all x1, starting transfers between devices, shards(): lax.all_to_all(split_grad, 'ctx', split_axis=2, concat_axis=4, tiled=True)  16.3 us
  transfers between devices with their start and end apart: 5, of which 3 were waited for; matrix products, arithmetic and copies ran while one was open for 3% of the time, Pallas kernels for 0%

profile of v1, /device:TPU:14, one launch (start us, length us, event | category | flops | bytes accessed | tf_op | source)
XLA Modules:
  0.0 577.9 jit_solution(10288572109656154985)
XLA Ops:
  7.2 2.5 copy.11
  9.7 16.3 %all-to-all-start = ((f32[1,8,64,4,128]{4,3,1,0,2:T(4,128)}), f32[1,8,64,4,128]{4,3,1,0,2:T(4,128)S(1)}, u32[]{:S(2)}, u32[]{:S(2)}) async-start(f32[1,8,64,4,128]{4,3,1,0,2:T(4,128)} %copy.11), calls=%async_computation | async-start | bytes 2097152 | tf_op jit(solution)/shard_map/all_to_all | solution.py:142
  27.3 49.3 %all-to-all-done = f32[1,8,64,4,128]{4,3,1,0,2:T(4,128)S(1)} async-done(((f32[1,8,64,4,128]{4,3,1,0,2:T(4,128)}), f32[1,8,64,4,128]{4,3,1,0,2:T(4,128)S(1)}, u32[]{:S(2)}, u32[]{:S(2)}) %all-to-all-start) | async-done | bytes 1048608 | tf_op jit(solution)/shard_map/all_to_all | solution.py:142
  76.6 9.0 %all-to-all-start.2 = ((f32[1,8,64,4,128]{4,3,1,0,2:T(4,128)}), f32[1,8,64,4,128]{4,3,1,0,2:T(4,128)}, u32[]{:S(2)}, u32[]{:S(2)}) async-start(f32[1,8,64,4,128]{4,3,1,0,2:T(4,128)} %copy.14), calls=%async_computation.2 | async-start | bytes 2097152 | tf_op jit(solution)/shard_map/all_to_all | solution.py:141
  88.7 99.1 %all-gather.3.cloned.1.call-done = f32[8,4,8192]{2,1,0:T(4,128)} async-done(((f32[1,4,8192]{2,1,0:T(4,128)}), f32[8,4,8192]{2,1,0:T(4,128)}) %all-gather.3.cloned.1.call-update) | async-done | bytes 1048592 | tf_op jit(solution)/shard_map/all_gather | solution.py:145
  187.7 1.9 reshape.86
  189.7 2.0 convolution_bitcast_fusion.1
  192.3 3.4 convolution_bitcast_fusion.2
  195.7 1.8 copy.15
  197.6 2.0 convolution_bitcast_fusion
  200.6 2.3 fusion.31
  202.9 2.1 fusion.34
  205.0 2.1 fusion.28
  207.9 2.1 fusion.8
  210.0 2.1 fusion.16
  212.8 1.5 fusion.46
  214.3 1.4 reshape_reshape.13
  218.3 1.3 constant_dynamic-update-slice_fusion.61
  222.3 1.3 constant_dynamic-update-slice_fusion.58
  223.6 1.3 constant_dynamic-update-slice_fusion.57
  224.9 1.3 constant_dynamic-update-slice_fusion.56
  230.2 1.3 constant_dynamic-update-slice_fusion.52
  232.8 1.3 constant_dynamic-update-slice_fusion.50
  236.8 1.3 constant_dynamic-update-slice_fusion.47
  242.0 1.3 constant_dynamic-update-slice_fusion.43
  243.4 1.3 constant_dynamic-update-slice_fusion.42
  244.7 1.3 constant_dynamic-update-slice_fusion.41
  248.6 1.3 constant_dynamic-update-slice_fusion.38
  250.0 1.3 constant_dynamic-update-slice_fusion.37
  255.2 1.3 constant_dynamic-update-slice_fusion.33
  257.9 1.3 constant_dynamic-update-slice_fusion.31
  263.1 1.3 constant_dynamic-update-slice_fusion.27
  264.4 1.3 constant_dynamic-update-slice_fusion.26
  265.8 1.3 constant_dynamic-update-slice_fusion.25
  268.4 1.3 constant_dynamic-update-slice_fusion.23
  269.7 1.3 constant_dynamic-update-slice_fusion.22
  271.0 1.3 constant_dynamic-update-slice_fusion.21
  281.6 1.3 constant_dynamic-update-slice_fusion.13
  282.9 1.3 constant_dynamic-update-slice_fusion.12
  285.5 1.3 constant_dynamic-update-slice_fusion.10
  289.5 1.3 constant_dynamic-update-slice_fusion.7
  292.1 1.3 constant_dynamic-update-slice_fusion.5
  293.4 1.3 constant_dynamic-update-slice_fusion.4
  300.0 5.8 all-to-all-start.1
  305.8 2.4 fusion.40
  308.3 2.6 mul.580
  312.2 255.5 %all-reduce.3.cloned.1.call-done = f32[8,4,8192]{2,1,0:T(4,128)} async-done(((f32[8,4,8192]{2,1,0:T(4,128)}), f32[8,4,8192]{2,1,0:T(4,128)}) %all-reduce.3.cloned.1.call-update) | async-done | bytes 1048592
  567.7 2.2 dynamic-slice_bitcast_fusion
  (73 shorter events, 59.8 us)
Async XLA Ops:
  9.7 16.3 %copy-start.3 = (f32[1,2048,128]{2,1,0:T(8,128)S(1)}, f32[1,2048,128]{2,1,0:T(8,128)}, u32[]{:S(2)}) copy-start(f32[1,2048,128]{2,1,0:T(8,128)} %param.3) | copy-start | bytes 3145732
  9.7 66.9 %all-to-all-start = ((f32[1,8,64,4,128]{4,3,1,0,2:T(4,128)}), f32[1,8,64,4,128]{4,3,1,0,2:T(4,128)S(1)}, u32[]{:S(2)}, u32[]{:S(2)}) async-start(f32[1,8,64,4,128]{4,3,1,0,2:T(4,128)} %copy.11), calls=%async_computation | async-start | bytes 2097152 | tf_op jit(solution)/shard_map/all_to_all | solution.py:142
  76.6 10.2 %copy-start.1 = (f32[1,8,64,4,128]{4,3,1,0,2:T(4,128)}, f32[1,8,64,4,128]{4,3,1,0,2:T(4,128)S(1)}, u32[]{:S(2)}) copy-start(f32[1,8,64,4,128]{4,3,1,0,2:T(4,128)S(1)} %all-to-all-done) | copy-start | bytes 3145732
  76.6 119.1 %all-to-all-start.2 = ((f32[1,8,64,4,128]{4,3,1,0,2:T(4,128)}), f32[1,8,64,4,128]{4,3,1,0,2:T(4,128)}, u32[]{:S(2)}, u32[]{:S(2)}) async-start(f32[1,8,64,4,128]{4,3,1,0,2:T(4,128)} %copy.14), calls=%async_computation.2 | async-start | bytes 2097152 | tf_op jit(solution)/shard_map/all_to_all | solution.py:141
  85.6 102.1 %all-gather.3.cloned.1.call-start = ((), (), s32[]{:S(2)}) async-start(), calls=%async_computation.3 | async-start | bytes 1179648 | tf_op jit(solution)/shard_map/all_gather | solution.py:145
  189.7 2.0 copy-start.2
  197.6 2.1 copy-start
  197.6 2.1 copy-start.4
  197.6 2.1 copy-start.5
  212.1 0.8 copy-start.6
  212.1 0.8 copy-start.7
  300.0 269.9 %all-to-all-start.1 = ((f32[64,1,8,1,4,128]{5,4,2,3,1,0:T(4,128)}), f32[64,1,8,1,4,128]{5,4,2,3,1,0:T(4,128)S(1)}, u32[]{:S(2)}, u32[]{:S(2)}) async-start(f32[64,1,8,1,4,128]{5,4,2,3,1,0:T(4,128)} %constant_dynamic-update-slice_fusion), calls=%async_computation.1 | async-start | bytes 2097152 | tf_op jit(solution)/shard_map/all_to_all | solution.py:172
  305.8 261.9 %all-reduce.3.cloned.1.call-start = ((), (), s32[]{:S(2)}) async-start(), calls=%async_computation.4 | async-start | bytes 2097152
Sparse Core Ops, SparseCore 0:
  89.7 97.9 all-gather.2
  311.0 256.6 all-reduce.2
